TPU v7x, 32 devices: a whole 2x2x4 slice. The times are simulated.
32 devices in a mesh: crop: 1, row: 16 (over z, y, core), col: 2 (over x).
Axes of the slice: x: 2, y: 2, z: 4, core: 2. Of those that a mesh axis runs over, the one named last changes fastest.
Arguments:
- pair: bfloat16 [256, 256, 128], P(('crop', 'row'), 'col'), may hold values from -6 to 6
- norm_gain: float32 [128], replicated, may hold values from 0.1 to 1.9
- norm_bias: float32 [128], replicated, may hold values from -3 to 3
- left_weight: bfloat16 [128, 256], replicated, may hold values from -0.5 to 0.5
- right_weight: bfloat16 [128, 256], replicated, may hold values from -0.5 to 0.5
- gate_weight: bfloat16 [128, 128], replicated, may hold values from -0.5 to 0.5
- out_gain: float32 [128], replicated, may hold values from 0.1 to 1.9
- out_bias: float32 [128], replicated, may hold values from -3 to 3
- out_weight: bfloat16 [128, 128], replicated, may hold values from -0.5 to 0.5
Outputs:
- update: bfloat16 [256, 256, 128], P(('crop', 'row'), 'col')
All inputs are finite; a program needn't handle non-finite values.
Results may differ from a plain program's by a relative error of at most 0.0085.
Values may be sent and summed in bfloat16 or wider, within the bound.
A program may use at most 64 MiB of HBM per device.

v0:
```python
import jax
import jax.numpy as jnp
from jax import lax
from jax.sharding import PartitionSpec as P


def body(
    pair,
    norm_gain,
    norm_bias,
    left_weight,
    right_weight,
    gate_weight,
    out_gain,
    out_bias,
    out_weight,
):
    hidden = out_gain.shape[0]
    values = pair.astype(jnp.float32)
    average = jnp.mean(values, axis=-1, keepdims=True)
    centred = values - average
    variance = jnp.mean(centred * centred, axis=-1, keepdims=True)
    normed = (centred * lax.rsqrt(variance + 1e-05) * norm_gain + norm_bias).astype(jnp.bfloat16)

    def branch(weight):
        projected = jnp.einsum("kic,cd->dki", normed, weight, preferred_element_type=jnp.float32)
        return (jax.nn.sigmoid(projected[hidden:]) * projected[:hidden]).astype(jnp.bfloat16)

    left = branch(left_weight)
    right = branch(right_weight)
    left_mine, right_mine = (
        lax.all_to_all(left, "row", split_axis=0, concat_axis=1, tiled=True),
        lax.all_to_all(right, "row", split_axis=0, concat_axis=1, tiled=True),
    )
    gate = jax.nn.sigmoid(
        jnp.einsum("kic,cd->kid", normed, gate_weight, preferred_element_type=jnp.float32)
    ).astype(jnp.bfloat16)
    product = jnp.einsum(
        "hki,hkj->hij",
        lax.all_gather(left_mine, "col", axis=2, tiled=True),
        right_mine,
        preferred_element_type=jnp.float32,
    ).astype(jnp.bfloat16)
    returned = lax.all_to_all(product, "row", split_axis=1, concat_axis=0, tiled=True)
    stats_in = returned.astype(jnp.float32)
    out_average = jnp.mean(stats_in, axis=0, keepdims=True)
    out_centred = stats_in - out_average
    out_variance = jnp.mean(out_centred * out_centred, axis=0, keepdims=True)
    normed_out = (
        out_centred * lax.rsqrt(out_variance + 1e-05) * out_gain[:, None, None]
        + out_bias[:, None, None]
    ).astype(jnp.bfloat16)
    projected_out = jnp.einsum(
        "hij,hd->ijd", normed_out, out_weight, preferred_element_type=jnp.float32
    )
    return (gate.astype(jnp.float32) * projected_out).astype(jnp.bfloat16)


def solution(mesh):
    in_specs = (P(("crop", "row"), "col", None), P(), P(), P(), P(), P(), P(), P(), P())
    out_specs = P(("crop", "row"), "col", None)
    return jax.shard_map(body, mesh=mesh, in_specs=in_specs, out_specs=out_specs, check_vma=False)
```

profile of v0, /device:TPU:0, one launch (start us, length us, event | category | flops | bytes accessed | tf_op | source)
XLA Modules:
  0.0 90.7 jit_solution(13841778811075401191)
XLA Ops:
  6.5 0.0 copy-start
  6.5 1.3 %convert_reduce_fusion = f32[16,128]{1,0:T(8,128)S(1)} fusion(bf16[16,128,128]{2,1,0:T(8,128)(2,1)} %param.9), kind=kLoop, calls=%fused_computation.8 | loop fusion | flops 522240 | bytes 532480 | tf_op jit(solution)/shard_map/reduce_sum | solution.py:20
  7.8 1.7 %fusion.8 = f32[16,128]{1,0:T(8,128)S(1)} fusion(bf16[16,128,128]{2,1,0:T(8,128)(2,1)} %param.9, f32[16,128]{1,0:T(8,128)S(1)} %broadcast_multiply_fusion.1), kind=kLoop, calls=%fused_computation.15 | loop fusion | flops 1046528 | bytes 540672 | tf_op jit(solution)/shard_map/reduce_sum | solution.py:22
  9.5 0.0 copy-done
  9.5 2.0 %convolution_bitcast_fusion.1 = f32[256,16,128]{0,2,1:T(8,128)S(1)} fusion(bf16[128,256]{1,0:T(8,128)(2,1)S(1)} %copy-done, bf16[16,128,128]{2,1,0:T(8,128)(2,1)} %param.9, f32[128]{0:T(128)} %param.11, f32[128]{0:T(128)} %param.10, f32[16,128]{1,0:T(8,128)S(1)} %add_rsqrt_fusion.1, f32[16,128]{1,0:T(8,128)S(1)} %broadcast_multiply_fusion.1), kind=kOutput, calls=%fused_computation.1 | convolution fusion | flops 135790592 | bytes 2704384 | tf_op jit(solution)/shard_map/kic,cd->dki/dot_general | solution.py:26
  11.5 0.0 copy-start.1
  11.5 0.0 copy-start.2
  11.5 0.0 copy-start.4
  11.5 0.0 copy-start.5
  11.6 0.3 fusion.16
  11.8 1.2 %copy.27 = bf16[128,16,128]{2,1,0:T(8,128)(2,1)} copy(bf16[128,16,128]{0,2,1:T(8,128)(2,1)S(1)} %fusion.16) | data formatting | bytes 1048576 | tf_op jit(solution)/shard_map/convert_element_type | solution.py:27
  13.0 7.4 %all-to-all-start = ((bf16[128,16,128]{2,1,0:T(8,128)(2,1)}), bf16[128,16,128]{2,1,0:T(8,128)(2,1)S(1)}, u32[]{:S(2)}, u32[]{:S(2)}) async-start(bf16[128,16,128]{2,1,0:T(8,128)(2,1)} %copy.27), calls=%async_computation | async-start | bytes 1048576 | tf_op jit(solution)/shard_map/all_to_all | solution.py:32
  20.4 0.0 all-gather.2.cloned.1.call-start
  20.5 0.0 copy-done.1
  20.5 0.0 copy-done.2
  20.5 0.0 copy-done.4
  20.5 0.0 copy-done.5
  20.5 0.7 convolution_bitcast_fusion
  21.3 13.6 %all-to-all-done = bf16[128,16,128]{2,1,0:T(8,128)(2,1)S(1)} async-done(((bf16[128,16,128]{2,1,0:T(8,128)(2,1)}), bf16[128,16,128]{2,1,0:T(8,128)(2,1)S(1)}, u32[]{:S(2)}, u32[]{:S(2)}) %all-to-all-start) | async-done | bytes 524320 | tf_op jit(solution)/shard_map/all_to_all | solution.py:32
  34.9 0.8 copy.28
  35.7 2.1 %copy.29 = bf16[8,256,128]{1,2,0:T(8,128)(2,1)} copy(bf16[8,256,128]{2,1,0:T(8,128)(2,1)} %bitcast.48) | data formatting | bytes 1048576 | tf_op jit(solution)/shard_map/all_to_all | solution.py:32
  37.8 0.0 all-gather.2.cloned.1.call-update
  37.8 0.3 fusion.12
  38.1 0.4 copy.30
  38.5 18.4 %all_to_all.45 = bf16[128,16,128]{2,1,0:T(8,128)(2,1)S(1)} all-to-all(bf16[128,16,128]{2,1,0:T(8,128)(2,1)S(1)} %copy.30), channel_id=1, replica_groups=mesh['crop'=1,'row'=16,'col'=2] {'row'}, dimensions={0} | all-to-all | bytes 1048576 | tf_op jit(solution)/shard_map/all_to_all | solution.py:33
  56.9 1.7 %all-gather.2.cloned.1.call-done = bf16[8,256,256]{1,2,0:T(8,128)(2,1)} async-done(((bf16[8,256,128]{1,2,0:T(8,128)(2,1)}), bf16[8,256,256]{1,2,0:T(8,128)(2,1)}) %all-gather.2.cloned.1.call-update) | async-done | bytes 1048592 | tf_op jit(solution)/shard_map/all_gather | solution.py:40
  58.7 0.0 copy-start.8
  58.7 1.6 %convolution_convert_fusion = bf16[8,256,128]{2,1,0:T(8,128)(2,1)S(1)} fusion(bf16[8,256,256]{1,2,0:T(8,128)(2,1)} %all-gather.2.cloned.1.call-done, bf16[8,256,128]{2,1,0:T(8,128)(2,1)S(1)} %bitcast.50), kind=kOutput, calls=%fused_computation.12 | convolution fusion | flops 134479872 | bytes 2097152 | tf_op jit(solution)/shard_map/hki,hkj->hij/dot_general | solution.py:38
  60.3 1.1 %copy.32 = bf16[8,256,128]{2,0,1:T(8,128)(2,1)} copy(bf16[8,256,128]{2,1,0:T(8,128)(2,1)S(1)} %convolution_convert_fusion) | data formatting | bytes 1048576 | tf_op jit(solution)/shard_map/convert_element_type | solution.py:43
  61.5 5.6 %all-to-all-start.2 = ((bf16[8,256,128]{2,0,1:T(8,128)(2,1)}), bf16[8,256,128]{2,0,1:T(8,128)(2,1)S(1)}, u32[]{:S(2)}, u32[]{:S(2)}) async-start(bf16[8,256,128]{2,0,1:T(8,128)(2,1)} %copy.32), calls=%async_computation.2 | async-start | bytes 1048576 | tf_op jit(solution)/shard_map/all_to_all | solution.py:44
  67.1 0.0 copy-done.8
  67.1 0.7 fusion.5
  67.9 13.7 %all-to-all-done.2 = bf16[8,256,128]{2,0,1:T(8,128)(2,1)S(1)} async-done(((bf16[8,256,128]{2,0,1:T(8,128)(2,1)}), bf16[8,256,128]{2,0,1:T(8,128)(2,1)S(1)}, u32[]{:S(2)}, u32[]{:S(2)}) %all-to-all-start.2) | async-done | bytes 524320 | tf_op jit(solution)/shard_map/all_to_all | solution.py:44
  81.6 0.2 fusion.33
  81.7 0.0 copy-start.6
  81.7 0.0 copy-start.7
  81.7 0.1 fusion.24
  81.9 0.0 copy-start.3
  81.9 0.2 multiply_reduce_fusion
  82.1 0.1 copy.34
  82.2 0.2 copy-done.6
  82.4 0.0 copy-done.7
  82.4 0.3 fusion.23
  82.7 0.0 copy-done.3
  82.8 1.1 %fusion.3 = bf16[16,128,128]{2,1,0:T(8,128)(2,1)} fusion(f32[16,128,128]{2,1,0:T(8,128)S(1)} %fusion.5, bf16[128,16,128]{2,1,0:T(8,128)(2,1)S(1)} %fusion.23, bf16[128,128]{1,0:T(8,128)(2,1)S(1)} %copy-done.3), kind=kOutput, calls=%fused_computation.9 | convolution fusion | flops 67633152 | bytes 2129920 | tf_op jit(solution)/shard_map/hij,hd->ijd/dot_general | solution.py:53
  (5 shorter events, 0.1 us)
Async XLA Ops:
  6.5 3.0 %copy-start = (bf16[128,256]{1,0:T(8,128)(2,1)S(1)}, bf16[128,256]{1,0:T(8,128)(2,1)}, u32[]{:S(2)}) copy-start(bf16[128,256]{1,0:T(8,128)(2,1)} %param.12) | copy-start | bytes 196612
  11.5 9.0 %copy-start.1 = (bf16[16,128,128]{2,1,0:T(8,128)(2,1)S(1)}, bf16[16,128,128]{2,1,0:T(8,128)(2,1)}, u32[]{:S(2)}) copy-start(bf16[16,128,128]{2,1,0:T(8,128)(2,1)} %param.9) | copy-start | bytes 1572868
  11.5 9.0 %copy-start.2 = (bf16[128,256]{1,0:T(8,128)(2,1)S(1)}, bf16[128,256]{1,0:T(8,128)(2,1)}, u32[]{:S(2)}) copy-start(bf16[128,256]{1,0:T(8,128)(2,1)} %param.13) | copy-start | bytes 196612
  11.5 9.0 %copy-start.4 = (f32[128]{0:T(128)S(1)}, f32[128]{0:T(128)}, u32[]{:S(2)}) copy-start(f32[128]{0:T(128)} %param.11) | copy-start | bytes 1540
  11.5 9.0 %copy-start.5 = (f32[128]{0:T(128)S(1)}, f32[128]{0:T(128)}, u32[]{:S(2)}) copy-start(f32[128]{0:T(128)} %param.10) | copy-start | bytes 1540
  13.0 21.9 %all-to-all-start = ((bf16[128,16,128]{2,1,0:T(8,128)(2,1)}), bf16[128,16,128]{2,1,0:T(8,128)(2,1)S(1)}, u32[]{:S(2)}, u32[]{:S(2)}) async-start(bf16[128,16,128]{2,1,0:T(8,128)(2,1)} %copy.27), calls=%async_computation | async-start | bytes 1048576 | tf_op jit(solution)/shard_map/all_to_all | solution.py:32
  20.4 38.2 %all-gather.2.cloned.1.call-start = ((), (), s32[]{:S(2)}) async-start(), calls=%async_computation.3 | async-start | bytes 1572864 | tf_op jit(solution)/shard_map/all_gather | solution.py:40
  58.7 8.4 %copy-start.8 = (bf16[128,128]{1,0:T(8,128)(2,1)S(1)}, bf16[128,128]{1,0:T(8,128)(2,1)}, u32[]{:S(2)}) copy-start(bf16[128,128]{1,0:T(8,128)(2,1)} %param.14) | copy-start | bytes 98308
  61.5 20.1 %all-to-all-start.2 = ((bf16[8,256,128]{2,0,1:T(8,128)(2,1)}), bf16[8,256,128]{2,0,1:T(8,128)(2,1)S(1)}, u32[]{:S(2)}, u32[]{:S(2)}) async-start(bf16[8,256,128]{2,0,1:T(8,128)(2,1)} %copy.32), calls=%async_computation.2 | async-start | bytes 1048576 | tf_op jit(solution)/shard_map/all_to_all | solution.py:44
  81.7 0.7 copy-start.6
  81.7 0.7 copy-start.7
  81.9 0.9 copy-start.3
Sparse Core Ops, SparseCore 0:
  37.9 20.7 all-gather.1
where the time goes:
time: 91.3 us; the launch traced here: 90.7 us
  waiting for transfers between devices  29.1 us (32%)
  blocking collectives  18.4 us (20%)
  between operations  13.6 us (15%)
  starting transfers between devices  13 us (14%)
  matrix products  6.22 us (7%)
  local copies, waits for them, and re-layouts  6.01 us (7%)
  other arithmetic  4.36 us (5%)
    all_to_all x1, blocking collectives, body(): lax.all_to_all(right, 'row', split_axis=0, concat_axis=1, tiled=True)  18.4 us
    all_to_all x1, waiting for transfers between devices, body(): lax.all_to_all(product, 'row', split_axis=1, concat_axis=0, tiled=True)  13.7 us
    all_to_all x1, waiting for transfers between devices, body(): lax.all_to_all(left, 'row', split_axis=0, concat_axis=1, tiled=True)  13.6 us
    all_to_all x1, starting transfers between devices, body(): lax.all_to_all(left, 'row', split_axis=0, concat_axis=1, tiled=True)  7.38 us
    all_to_all x1, starting transfers between devices, body(): lax.all_to_all(product, 'row', split_axis=1, concat_axis=0, tiled=True)  5.62 us
    all_to_all x2, local copies, waits for them, and re-layouts, body(): lax.all_to_all(left, 'row', split_axis=0, concat_axis=1, tiled=True)  2.88 us
    dot_general x2, matrix products, branch(): jnp.einsum('kic,cd->dki', normed, weight, preferred_element_type=jnp.floa...  2.69 us
  transfers between devices with their start and end apart: 3, of which 3 were waited for; matrix products, arithmetic and copies ran while one was open for 2% of the time, Pallas kernels for 0%

commit v1 on v0

--- a/solution.py
+++ b/solution.py
@@ -1,6 +1,10 @@
+import functools
+
 import jax
 import jax.numpy as jnp
 from jax import lax
+from jax.experimental import pallas as pl
+from jax.experimental.pallas import tpu as pltpu
 from jax.sharding import PartitionSpec as P
 
 
@@ -56,7 +60,249 @@
     return (gate.astype(jnp.float32) * projected_out).astype(jnp.bfloat16)
 
 
+MESH = pl.DeviceIdType.MESH
+CHUNKS = 2
+
+
+def sigmoid(x):
+    return 0.5 * jnp.tanh(0.5 * x) + 0.5
+
+
+def kernel(
+    rows,
+    cols,
+    pair_ref,
+    norm_gain_ref,
+    norm_bias_ref,
+    left_ref,
+    right_ref,
+    gate_weight_ref,
+    out_gain_ref,
+    out_bias_ref,
+    out_weight_ref,
+    out_ref,
+    normed,
+    weights,
+    staged,
+    operands_out,
+    operands_in,
+    product_out,
+    product_in,
+    centred,
+    gate,
+    send_sem,
+    recv_sem,
+    send_back_sem,
+    recv_back_sem,
+):
+    tok_row, tok_col, pair = pair_ref.shape
+    hidden = out_gain_ref.shape[1]
+    devices = rows * cols
+    turns = hidden // devices
+    per = turns // CHUNKS
+    part = per * devices
+    tokens = rows * tok_row
+    row, col = lax.axis_index("row"), lax.axis_index("col")
+    me = col * rows + row
+
+    def others(one):
+        def step(offset, carry):
+            other = lax.rem(me + offset, devices)
+            one(other, lax.rem(other, rows), lax.div(other, rows))
+            return carry
+
+        lax.fori_loop(1, devices, step, 0)
+
+    barrier = pltpu.get_barrier_semaphore()
+    others(
+        lambda other, r, c: pl.semaphore_signal(
+            barrier, inc=1, device_id={"row": r, "col": c}, device_id_type=MESH
+        )
+    )
+
+    gain, bias = norm_gain_ref[...], norm_bias_ref[...]
+    step_rows = 4
+    for k in range(0, tok_row, step_rows):
+        x = pair_ref[k : k + step_rows].reshape(step_rows * tok_col, pair).astype(jnp.float32)
+        average = jnp.mean(x, axis=-1, keepdims=True)
+        x = x - average
+        variance = jnp.mean(x * x, axis=-1, keepdims=True)
+        normed[k * tok_col : (k + step_rows) * tok_col] = (
+            x * lax.rsqrt(variance + 1e-05) * gain + bias
+        ).astype(jnp.bfloat16)
+
+    for side, ref in enumerate((left_ref, right_ref)):
+        turned = ref[...].astype(jnp.float32).T.astype(jnp.bfloat16)
+        for m in range(CHUNKS):
+            for half in range(2):
+                weights[m, (2 * side + half) * part : (2 * side + half + 1) * part] = turned[
+                    half * hidden + m * part : half * hidden + (m + 1) * part
+                ]
+
+    def operand_copy(m, other, r, c, slot):
+        sc, sr = slot
+        return pltpu.make_async_remote_copy(
+            src_ref=operands_out.at[pl.ds(m * per, per), other],
+            dst_ref=operands_in.at[pl.ds(m * per, per), sc, sr],
+            send_sem=send_sem.at[m, other],
+            recv_sem=recv_sem.at[m, sc * rows + sr],
+            device_id={"row": r, "col": c},
+            device_id_type=MESH,
+        )
+
+    def product_copy(m, other, r, c, slot):
+        return pltpu.make_async_remote_copy(
+            src_ref=product_out.at[pl.ds(m * per, per), c, r],
+            dst_ref=product_in.at[pl.ds(m * per, per), slot],
+            send_sem=send_back_sem.at[m, other],
+            recv_sem=recv_back_sem.at[m, slot],
+            device_id={"row": r, "col": c},
+            device_id_type=MESH,
+        )
+
+    for m in range(CHUNKS):
+        for k in range(0, tok_row, step_rows):
+            projected = lax.dot_general(
+                weights[m],
+                normed[k * tok_col : (k + step_rows) * tok_col],
+                (((1,), (1,)), ((), ())),
+                preferred_element_type=jnp.float32,
+            )
+            for side in range(2):
+                values = projected[2 * side * part : (2 * side + 1) * part]
+                gates = projected[(2 * side + 1) * part : (2 * side + 2) * part]
+                gated = sigmoid(gates) * values
+                for kk in range(step_rows):
+                    staged[side, :, k + kk, :] = gated[:, kk * tok_col : (kk + 1) * tok_col]
+        for side in range(2):
+            for t in range(per):
+                operands_out[m * per + t, :, side] = staged[
+                    side, t * devices : (t + 1) * devices
+                ].astype(jnp.bfloat16)
+        if m == 0:
+            pl.semaphore_wait(barrier, devices - 1)
+        others(lambda other, r, c: operand_copy(m, other, r, c, (col, row)).start())
+        for t in range(per):
+            q = m * per + t
+            operands_in[q, col, row] = operands_out[q, me]
+
+    for k in range(0, tok_row, step_rows):
+        gate[k * tok_col : (k + step_rows) * tok_col] = sigmoid(
+            jnp.dot(
+                normed[k * tok_col : (k + step_rows) * tok_col],
+                gate_weight_ref[...],
+                preferred_element_type=jnp.float32,
+            )
+        ).astype(jnp.bfloat16)
+
+    for m in range(CHUNKS):
+        others(lambda other, r, c: operand_copy(m, other, r, c, (c, r)).wait_recv())
+        for t in range(per):
+            q = m * per + t
+            left, right = (
+                jnp.concatenate(
+                    [operands_in[q, c, :, side].reshape(tokens, tok_col) for c in range(cols)],
+                    axis=1,
+                )
+                for side in range(2)
+            )
+            product = lax.dot_general(
+                left, right, (((0,), (0,)), ((), ())), preferred_element_type=jnp.float32
+            ).astype(jnp.bfloat16)
+            for c in range(cols):
+                product_out[q, c] = product[:, c * tok_col : (c + 1) * tok_col].reshape(
+                    rows, tok_row, tok_col
+                )
+        others(lambda other, r, c: product_copy(m, other, r, c, me).start())
+        for t in range(per):
+            q = m * per + t
+            product_in[q, me] = product_out[q, col, row]
+
+    def across(ref):
+        return jnp.broadcast_to(ref[...], (tok_col, hidden)).T
+
+    out_gain, out_bias = across(out_gain_ref), across(out_bias_ref)
+    for m in range(CHUNKS):
+        others(lambda other, r, c: product_copy(m, other, r, c, other).wait_recv())
+
+    total = jnp.zeros((tok_row, tok_col), jnp.float32)
+    for q in range(turns):
+        total += jnp.sum(product_in[q].astype(jnp.float32), axis=0)
+    average = total * (1.0 / hidden)
+    squares = jnp.zeros((tok_row, tok_col), jnp.float32)
+    for q in range(turns):
+        x = product_in[q].astype(jnp.float32) - average
+        squares += jnp.sum(x * x, axis=0)
+        centred[q * devices : (q + 1) * devices] = x
+    scale = lax.rsqrt(squares * (1.0 / hidden) + 1e-05)
+    for i in range(tok_row):
+        x = centred[:, i, :] * scale[i : i + 1] * out_gain + out_bias
+        projected = lax.dot_general(
+            x.astype(jnp.bfloat16),
+            out_weight_ref[...],
+            (((0,), (0,)), ((), ())),
+            preferred_element_type=jnp.float32,
+        )
+        gates = gate[i * tok_col : (i + 1) * tok_col].astype(jnp.float32)
+        out_ref[i] = (gates * projected).astype(jnp.bfloat16)
+
+    for m in range(CHUNKS):
+        others(lambda other, r, c: operand_copy(m, other, r, c, (c, r)).wait_send())
+        others(lambda other, r, c: product_copy(m, other, r, c, other).wait_send())
+
+
+def fused(rows, cols, pair, norm_gain, norm_bias, left_weight, right_weight, gate_weight, out_gain, out_bias, out_weight):
+    tok_row, tok_col, channels = pair.shape
+    hidden = out_gain.shape[0]
+    devices = rows * cols
+    turns = hidden // devices
+    part = hidden // CHUNKS
+    bf16, f32 = jnp.bfloat16, jnp.float32
+    return pl.pallas_call(
+        functools.partial(kernel, rows, cols),
+        out_shape=jax.ShapeDtypeStruct(pair.shape, bf16),
+        in_specs=[pl.BlockSpec(memory_space=pltpu.VMEM)] * 9,
+        out_specs=pl.BlockSpec(memory_space=pltpu.VMEM),
+        scratch_shapes=[
+            pltpu.VMEM((tok_row * tok_col, channels), bf16),
+            pltpu.VMEM((CHUNKS, 4 * part, channels), bf16),
+            pltpu.VMEM((2, part, tok_row, tok_col), f32),
+            pltpu.VMEM((turns, devices, 2, tok_row, tok_col), bf16),
+            pltpu.VMEM((turns, cols, rows, 2, tok_row, tok_col), bf16),
+            pltpu.VMEM((turns, cols, rows, tok_row, tok_col), bf16),
+            pltpu.VMEM((turns, devices, tok_row, tok_col), bf16),
+            pltpu.VMEM((hidden, tok_row, tok_col), f32),
+            pltpu.VMEM((tok_row * tok_col, channels), bf16),
+            pltpu.SemaphoreType.DMA((CHUNKS, devices)),
+            pltpu.SemaphoreType.DMA((CHUNKS, devices)),
+            pltpu.SemaphoreType.DMA((CHUNKS, devices)),
+            pltpu.SemaphoreType.DMA((CHUNKS, devices)),
+        ],
+        compiler_params=pltpu.CompilerParams(
+            collective_id=0, has_side_effects=True, vmem_limit_bytes=40 * 2**20
+        ),
+    )(
+        pair,
+        norm_gain[None],
+        norm_bias[None],
+        left_weight,
+        right_weight,
+        gate_weight,
+        out_gain[None],
+        out_bias[None],
+        out_weight,
+    )
+
+
 def solution(mesh):
     in_specs = (P(("crop", "row"), "col", None), P(), P(), P(), P(), P(), P(), P(), P())
     out_specs = P(("crop", "row"), "col", None)
-    return jax.shard_map(body, mesh=mesh, in_specs=in_specs, out_specs=out_specs, check_vma=False)
+    rows, cols = mesh.shape["row"], mesh.shape["col"]
+
+    def local(pair, norm_gain, *rest):
+        hidden = rest[4].shape[0]
+        if hidden % (rows * cols * CHUNKS) == 0:
+            return fused(rows, cols, pair, norm_gain, *rest)
+        return body(pair, norm_gain, *rest)
+
+    return jax.shard_map(local, mesh=mesh, in_specs=in_specs, out_specs=out_specs, check_vma=False)

time: 91.3 us -> 52.3 us (0.57)
  Pallas kernels: 0 us -> 46.2 us
  waiting for transfers between devices: 29.1 us -> 0 us
  blocking collectives: 18.4 us -> 0 us
  between operations: 13.6 us -> 0.02 us
  starting transfers between devices: 13 us -> 0 us
  matrix products: 6.22 us -> 0 us
  other arithmetic: 4.36 us -> 0 us
    pallas_call x0 -> x1, Pallas kernels: none -> 46.2 us  [fused(): pl.pallas_call(functools.partial(kernel, rows, cols), out_shape=jax.Shape...]
    all_to_all x2 -> x0, waiting for transfers between devices: 27.3 us -> none  [the longest x1 13.7 us: body(): lax.all_to_all(product, 'row', split_axis=1, concat_axis=0, tiled=True)]
    all_to_all x1 -> x0, blocking collectives: 18.4 us -> none  [body(): lax.all_to_all(right, 'row', split_axis=0, concat_axis=1, tiled=True)]
    all_to_all x2 -> x0, starting transfers between devices: 13 us -> none  [the longest x1 7.38 us: body(): lax.all_to_all(left, 'row', split_axis=0, concat_axis=1, tiled=True)]
    dot_general x5 -> x0, matrix products: 6.22 us -> none  [the longest x2 2.69 us: branch(): jnp.einsum('kic,cd->dki', normed, weight, preferred_element_type=jnp.floa...]
    unnamed x18 -> x19, local copies, waits for them, and re-layouts: 0.23 us -> 5.73 us
    reduce_sum x4 -> x0, other arithmetic: 3.28 us -> none  [the longest x1 1.67 us: body(): variance = jnp.mean(centred * centred, axis=-1, keepdims=True)]
    all_to_all x3 -> x0, local copies, waits for them, and re-layouts: 2.91 us -> none  [the longest x2 2.88 us: body(): lax.all_to_all(left, 'row', split_axis=0, concat_axis=1, tiled=True)]
  transfers between devices with their start and end apart: 3 -> 0, of which waited for: 3 -> 0; matrix products, arithmetic and copies ran while one was open for 2% -> 0% of each run, Pallas kernels for 0% -> 0%
where the time goes in v1:
time: 52.3 us; the launch traced here: 51.9 us
  Pallas kernels  46.2 us (88%)
  local copies, waits for them, and re-layouts  5.73 us (11%)
    pallas_call x1, Pallas kernels, fused(): pl.pallas_call(functools.partial(kernel, rows, cols), out_shape=jax.Shape...  46.2 us
    unnamed x19, local copies, waits for them, and re-layouts  5.73 us

profile of v1, /device:TPU:0, one launch (start us, length us, event | category | flops | bytes accessed | tf_op | source)
XLA Modules:
  0.0 51.9 jit_solution(10184789963262526135)
XLA Ops:
  0.0 0.0 copy-start.8
  0.0 0.0 copy-start.5
  0.0 0.0 copy-start.6
  0.0 0.0 copy-start.7
  0.0 0.6 %copy-done.8 = f32[128]{0:T(128)S(1)} copy-done((f32[128]{0:T(128)S(1)}, f32[128]{0:T(128)}, u32[]{:S(2)}) %copy-start.8) | copy-done | bytes 536
  0.7 0.0 copy-done.5
  0.7 0.0 copy-done.6
  0.7 0.0 copy-done.7
  0.7 0.0 copy-start
  0.7 1.0 %copy-done = bf16[16,128,128]{2,1,0:T(8,128)(2,1)S(1)} copy-done((bf16[16,128,128]{2,1,0:T(8,128)(2,1)S(1)}, bf16[16,128,128]{2,1,0:T(8,128)(2,1)}, u32[]{:S(2)}) %copy-start) | copy-done | bytes 524312
  1.7 0.0 copy-start.1
  1.7 0.8 %copy-done.1 = bf16[128,256]{1,0:T(8,128)(2,1)S(1)} copy-done((bf16[128,256]{1,0:T(8,128)(2,1)S(1)}, bf16[128,256]{1,0:T(8,128)(2,1)}, u32[]{:S(2)}) %copy-start.1) | copy-done | bytes 65560
  2.6 0.0 copy-start.2
  2.6 0.8 %copy-done.2 = bf16[128,256]{1,0:T(8,128)(2,1)S(1)} copy-done((bf16[128,256]{1,0:T(8,128)(2,1)S(1)}, bf16[128,256]{1,0:T(8,128)(2,1)}, u32[]{:S(2)}) %copy-start.2) | copy-done | bytes 65560
  3.4 0.0 copy-start.3
  3.4 0.8 %copy-done.3 = bf16[128,128]{1,0:T(8,128)(2,1)S(1)} copy-done((bf16[128,128]{1,0:T(8,128)(2,1)S(1)}, bf16[128,128]{1,0:T(8,128)(2,1)}, u32[]{:S(2)}) %copy-start.3) | copy-done | bytes 32792
  4.2 0.0 copy-start.4
  4.2 0.8 %copy-done.4 = bf16[128,128]{1,0:T(8,128)(2,1)S(1)} copy-done((bf16[128,128]{1,0:T(8,128)(2,1)S(1)}, bf16[128,128]{1,0:T(8,128)(2,1)}, u32[]{:S(2)}) %copy-start.4) | copy-done | bytes 32792
  4.9 46.2 %shard_map.91 = bf16[16,128,128]{2,1,0:T(8,128)(2,1)S(1)} custom-call(bf16[16,128,128]{2,1,0:T(8,128)(2,1)S(1)} %copy-done, f32[1,128]{1,0:T(1,128)S(1)} %bitcast.4, f32[1,128]{1,0:T(1,128)S(1)} %bitcast.5, bf16[128,256]{1,0:T(8,128)(2,1)S(1)} %copy-done.1, bf16[128,256]{1,0:T(8,128)(2,1)S(1)} %copy-done.2, bf16[128,128]{1,0:T(8,128)(2,1)S(1)} %copy-done.3, ...), custom_call_target="tpu_custom_call" | custom-call | tf_op jit(solution)/shard_map/pallas_call | solution.py:261
  51.1 0.8 %copy.11 = bf16[16,128,128]{2,1,0:T(8,128)(2,1)} copy(bf16[16,128,128]{2,1,0:T(8,128)(2,1)S(1)} %shard_map.91) | data formatting | bytes 1048576
Async XLA Ops:
  0.0 0.7 %copy-start.8 = (f32[128]{0:T(128)S(1)}, f32[128]{0:T(128)}, u32[]{:S(2)}) copy-start(f32[128]{0:T(128)} %param.16) | copy-start | bytes 1540
  0.0 0.7 %copy-start.5 = (f32[128]{0:T(128)S(1)}, f32[128]{0:T(128)}, u32[]{:S(2)}) copy-start(f32[128]{0:T(128)} %param.10) | copy-start | bytes 1540
  0.0 0.7 %copy-start.6 = (f32[128]{0:T(128)S(1)}, f32[128]{0:T(128)}, u32[]{:S(2)}) copy-start(f32[128]{0:T(128)} %param.11) | copy-start | bytes 1540
  0.0 0.7 %copy-start.7 = (f32[128]{0:T(128)S(1)}, f32[128]{0:T(128)}, u32[]{:S(2)}) copy-start(f32[128]{0:T(128)} %param.15) | copy-start | bytes 1540
  0.7 1.0 %copy-start = (bf16[16,128,128]{2,1,0:T(8,128)(2,1)S(1)}, bf16[16,128,128]{2,1,0:T(8,128)(2,1)}, u32[]{:S(2)}) copy-start(bf16[16,128,128]{2,1,0:T(8,128)(2,1)} %pair_ref.1) | copy-start | bytes 1572868
  1.7 0.8 %copy-start.1 = (bf16[128,256]{1,0:T(8,128)(2,1)S(1)}, bf16[128,256]{1,0:T(8,128)(2,1)}, u32[]{:S(2)}) copy-start(bf16[128,256]{1,0:T(8,128)(2,1)} %left_ref.1) | copy-start | bytes 196612
  2.6 0.8 %copy-start.2 = (bf16[128,256]{1,0:T(8,128)(2,1)S(1)}, bf16[128,256]{1,0:T(8,128)(2,1)}, u32[]{:S(2)}) copy-start(bf16[128,256]{1,0:T(8,128)(2,1)} %right_ref.1) | copy-start | bytes 196612
  3.4 0.8 %copy-start.3 = (bf16[128,128]{1,0:T(8,128)(2,1)S(1)}, bf16[128,128]{1,0:T(8,128)(2,1)}, u32[]{:S(2)}) copy-start(bf16[128,128]{1,0:T(8,128)(2,1)} %gate_weight_ref.1) | copy-start | bytes 98308
  4.2 0.8 %copy-start.4 = (bf16[128,128]{1,0:T(8,128)(2,1)S(1)}, bf16[128,128]{1,0:T(8,128)(2,1)}, u32[]{:S(2)}) copy-start(bf16[128,128]{1,0:T(8,128)(2,1)} %out_weight_ref.1) | copy-start | bytes 98308

commit v2 on v0

--- a/solution.py
+++ b/solution.py
@@ -1,6 +1,10 @@
+import functools
+
 import jax
 import jax.numpy as jnp
 from jax import lax
+from jax.experimental import pallas as pl
+from jax.experimental.pallas import tpu as pltpu
 from jax.sharding import PartitionSpec as P
 
 
@@ -56,7 +60,309 @@
     return (gate.astype(jnp.float32) * projected_out).astype(jnp.bfloat16)
 
 
+MESH = pl.DeviceIdType.MESH
+CHUNKS = 4
+UNROLL = 1
+PACED = False
+HALVES = 2
+
+
+def sigmoid(x):
+    return 0.5 * jnp.tanh(0.5 * x) + 0.5
+
+
+def kernel(rows, cols, *refs):
+    arguments, out_ref = refs[:9], refs[9]
+    held = refs[10:19]
+    (
+        normed,
+        weights,
+        staged,
+        operands_out,
+        operands_in,
+        product_out,
+        product_in,
+        centred,
+        gate,
+        fetch_sem,
+        send_sem,
+        recv_sem,
+        send_back_sem,
+        recv_back_sem,
+    ) = refs[19:]
+    fetches = [
+        pltpu.make_async_copy(source, target, fetch_sem.at[n])
+        for n, (source, target) in enumerate(zip(arguments, held))
+    ]
+    for fetch in fetches:
+        fetch.start()
+    (
+        pair_ref,
+        norm_gain_ref,
+        norm_bias_ref,
+        left_ref,
+        right_ref,
+        gate_weight_ref,
+        out_gain_ref,
+        out_bias_ref,
+        out_weight_ref,
+    ) = held
+    tok_row, tok_col, pair = pair_ref.shape
+    hidden = out_gain_ref.shape[1]
+    half_rows = rows // HALVES
+    members = half_rows * cols
+    turns = hidden // members
+    per = turns // CHUNKS
+    part = per * members
+    half_tokens = half_rows * tok_row
+    row, col = lax.axis_index("row"), lax.axis_index("col")
+    half, half_row = lax.div(row, half_rows), lax.rem(row, half_rows)
+    me = col * half_rows + half_row
+
+    def near(one):
+        def step(offset, carry):
+            other = lax.rem(me + offset, members)
+            one(half, other, lax.rem(other, half_rows), lax.div(other, half_rows))
+            return carry
+
+        lax.fori_loop(1, members, step, 0, unroll=UNROLL)
+
+    def far(one):
+        for away in range(1, HALVES):
+
+            def step(offset, carry):
+                other = lax.rem(me + offset, members)
+                one(
+                    lax.rem(half + away, HALVES),
+                    other,
+                    lax.rem(other, half_rows),
+                    lax.div(other, half_rows),
+                )
+                return carry
+
+            lax.fori_loop(0, members, step, 0, unroll=UNROLL)
+
+    def everyone(one):
+        far(one)
+        near(one)
+
+    def place(h, r, c):
+        return {"row": h * half_rows + r, "col": c}
+
+    barrier = pltpu.get_barrier_semaphore()
+    everyone(
+        lambda h, other, r, c: pl.semaphore_signal(
+            barrier, inc=1, device_id=place(h, r, c), device_id_type=MESH
+        )
+    )
+    for fetch in fetches:
+        fetch.wait()
+
+    gain, bias = norm_gain_ref[...], norm_bias_ref[...]
+    step_rows = 4
+    for k in range(0, tok_row, step_rows):
+        x = pair_ref[k : k + step_rows].reshape(step_rows * tok_col, pair).astype(jnp.float32)
+        average = jnp.mean(x, axis=-1, keepdims=True)
+        x = x - average
+        variance = jnp.mean(x * x, axis=-1, keepdims=True)
+        normed[k * tok_col : (k + step_rows) * tok_col] = (
+            x * lax.rsqrt(variance + 1e-05) * gain + bias
+        ).astype(jnp.bfloat16)
+
+    for side, ref in enumerate((left_ref, right_ref)):
+        turned = ref[...].astype(jnp.float32).T.astype(jnp.bfloat16)
+        for m in range(CHUNKS):
+            for piece in range(2):
+                weights[m, (2 * side + piece) * part : (2 * side + piece + 1) * part] = turned[
+                    piece * hidden + m * part : piece * hidden + (m + 1) * part
+                ]
+
+    def operand_copy(m, h, other, r, c, slot):
+        return pltpu.make_async_remote_copy(
+            src_ref=operands_out.at[pl.ds(m * per, per), other],
+            dst_ref=operands_in.at[pl.ds(m * per, per), slot],
+            send_sem=send_sem.at[m],
+            recv_sem=recv_sem.at[m],
+            device_id=place(h, r, c),
+            device_id_type=MESH,
+        )
+
+    def product_copy(m, h, other, r, c, slot):
+        return pltpu.make_async_remote_copy(
+            src_ref=product_out.at[pl.ds(m * per, per), c, h * half_rows + r],
+            dst_ref=product_in.at[pl.ds(m * per, per), slot],
+            send_sem=send_back_sem.at[m],
+            recv_sem=recv_back_sem.at[m],
+            device_id=place(h, r, c),
+            device_id_type=MESH,
+        )
+
+    def arrived(ref, m, blocks, sem):
+        all_blocks = ref.at[pl.ds(m * per, per), pl.ds(0, blocks)]
+        pltpu.make_async_copy(all_blocks, all_blocks, sem.at[m]).wait()
+
+    def project(m):
+        for k in range(0, tok_row, step_rows):
+            projected = lax.dot_general(
+                weights[m],
+                normed[k * tok_col : (k + step_rows) * tok_col],
+                (((1,), (1,)), ((), ())),
+                preferred_element_type=jnp.float32,
+            )
+            for side in range(2):
+                values = projected[2 * side * part : (2 * side + 1) * part]
+                gates = projected[(2 * side + 1) * part : (2 * side + 2) * part]
+                gated = sigmoid(gates) * values
+                for kk in range(step_rows):
+                    staged[side, :, k + kk, :] = gated[:, kk * tok_col : (kk + 1) * tok_col]
+        for side in range(2):
+            for t in range(per):
+                operands_out[m * per + t, :, side] = staged[
+                    side, t * members : (t + 1) * members
+                ].astype(jnp.bfloat16)
+
+    def send_operands(m):
+        near(lambda h, other, r, c: operand_copy(m, h, other, r, c, me).start())
+        for t in range(per):
+            q = m * per + t
+            operands_in[q, me] = operands_out[q, me]
+
+    project(0)
+    pl.semaphore_wait(barrier, HALVES * members - 1)
+    send_operands(0)
+    if not PACED:
+        for m in range(1, CHUNKS):
+            project(m)
+            send_operands(m)
+    for m in range(CHUNKS):
+        if PACED and m + 1 < CHUNKS:
+            project(m + 1)
+        arrived(operands_in, m, members - 1, recv_sem)
+        if PACED and m + 1 < CHUNKS:
+            send_operands(m + 1)
+        for t in range(per):
+            q = m * per + t
+            left, right = (
+                jnp.concatenate(
+                    [
+                        operands_in[q, c * half_rows : (c + 1) * half_rows, side].reshape(
+                            half_tokens, tok_col
+                        )
+                        for c in range(cols)
+                    ],
+                    axis=1,
+                )
+                for side in range(2)
+            )
+            product = lax.dot_general(
+                left, right, (((0,), (0,)), ((), ())), preferred_element_type=jnp.float32
+            ).astype(jnp.bfloat16)
+            for c in range(cols):
+                product_out[q, c] = product[:, c * tok_col : (c + 1) * tok_col].reshape(
+                    rows, tok_row, tok_col
+                )
+        everyone(lambda h, other, r, c: product_copy(m, h, other, r, c, half * members + me).start())
+        for t in range(per):
+            q = m * per + t
+            product_in[q, half * members + me] = product_out[q, col, row]
+
+    for k in range(0, tok_row, step_rows):
+        gate[k * tok_col : (k + step_rows) * tok_col] = sigmoid(
+            jnp.dot(
+                normed[k * tok_col : (k + step_rows) * tok_col],
+                gate_weight_ref[...],
+                preferred_element_type=jnp.float32,
+            )
+        ).astype(jnp.bfloat16)
+
+    def across(ref):
+        return jnp.broadcast_to(ref[...], (tok_col, hidden)).T
+
+    out_gain, out_bias = across(out_gain_ref), across(out_bias_ref)
+    averages, squares = [], []
+    for m in range(CHUNKS):
+        arrived(product_in, m, HALVES * members - 1, recv_back_sem)
+        total = jnp.zeros((tok_row, tok_col), jnp.float32)
+        for q in range(m * per, (m + 1) * per):
+            x = product_in[q, :members].astype(jnp.float32)
+            for h in range(1, HALVES):
+                x += product_in[q, h * members : (h + 1) * members].astype(jnp.float32)
+            centred[q * members : (q + 1) * members] = x
+            total += jnp.sum(x, axis=0)
+        average = total * (1.0 / part)
+        square = jnp.zeros((tok_row, tok_col), jnp.float32)
+        for q in range(m * per, (m + 1) * per):
+            x = centred[q * members : (q + 1) * members] - average
+            square += jnp.sum(x * x, axis=0)
+        averages.append(average)
+        squares.append(square)
+    average = sum(averages) * (1.0 / CHUNKS)
+    square = sum(squares)
+    for one in averages:
+        square += part * (one - average) * (one - average)
+    scale = lax.rsqrt(square * (1.0 / hidden) + 1e-05)
+    for i in range(tok_row):
+        x = (centred[:, i, :] - average[i : i + 1]) * scale[i : i + 1] * out_gain + out_bias
+        projected = lax.dot_general(
+            x.astype(jnp.bfloat16),
+            out_weight_ref[...],
+            (((0,), (0,)), ((), ())),
+            preferred_element_type=jnp.float32,
+        )
+        gates = gate[i * tok_col : (i + 1) * tok_col].astype(jnp.float32)
+        out_ref[i] = (gates * projected).astype(jnp.bfloat16)
+
+    for m in range(CHUNKS):
+        arrived(operands_in, m, members - 1, send_sem)
+        arrived(product_in, m, HALVES * members - 1, send_back_sem)
+
+
+def fused(rows, cols, *arguments):
+    arguments = [pltpu.with_memory_space_constraint(a[None] if a.ndim == 1 else a, pltpu.HBM) for a in arguments]
+    tok_row, tok_col, channels = arguments[0].shape
+    hidden = arguments[6].shape[1]
+    members = rows * cols // HALVES
+    turns = hidden // members
+    part = hidden // CHUNKS
+    bf16, f32 = jnp.bfloat16, jnp.float32
+    dma = pltpu.SemaphoreType.DMA
+    return pl.pallas_call(
+        functools.partial(kernel, rows, cols),
+        out_shape=jax.ShapeDtypeStruct(arguments[0].shape, bf16),
+        in_specs=[pl.BlockSpec(memory_space=pltpu.HBM)] * 9,
+        out_specs=pl.BlockSpec(memory_space=pltpu.VMEM),
+        scratch_shapes=[pltpu.VMEM(a.shape, a.dtype) for a in arguments]
+        + [
+            pltpu.VMEM((tok_row * tok_col, channels), bf16),
+            pltpu.VMEM((CHUNKS, 4 * part, channels), bf16),
+            pltpu.VMEM((2, part, tok_row, tok_col), f32),
+            pltpu.VMEM((turns, members, 2, tok_row, tok_col), bf16),
+            pltpu.VMEM((turns, members, 2, tok_row, tok_col), bf16),
+            pltpu.VMEM((turns, cols, rows, tok_row, tok_col), bf16),
+            pltpu.VMEM((turns, HALVES * members, tok_row, tok_col), bf16),
+            pltpu.VMEM((hidden, tok_row, tok_col), f32),
+            pltpu.VMEM((tok_row * tok_col, channels), bf16),
+            dma((9,)),
+            dma((CHUNKS,)),
+            dma((CHUNKS,)),
+            dma((CHUNKS,)),
+            dma((CHUNKS,)),
+        ],
+        compiler_params=pltpu.CompilerParams(
+            collective_id=0, has_side_effects=True, vmem_limit_bytes=40 * 2**20
+        ),
+    )(*arguments)
+
+
 def solution(mesh):
     in_specs = (P(("crop", "row"), "col", None), P(), P(), P(), P(), P(), P(), P(), P())
     out_specs = P(("crop", "row"), "col", None)
-    return jax.shard_map(body, mesh=mesh, in_specs=in_specs, out_specs=out_specs, check_vma=False)
+    rows, cols = mesh.shape["row"], mesh.shape["col"]
+
+    def local(*arguments):
+        channels = arguments[6].shape[0] * HALVES
+        if rows % HALVES == 0 and channels % (rows * cols * CHUNKS) == 0:
+            return fused(rows, cols, *arguments)
+        return body(*arguments)
+
+    return jax.shard_map(local, mesh=mesh, in_specs=in_specs, out_specs=out_specs, check_vma=False)

time: 91.3 us -> 39.8 us (0.44)
  Pallas kernels: 0 us -> 38.9 us
  waiting for transfers between devices: 29.1 us -> 0 us
  blocking collectives: 18.4 us -> 0 us
  between operations: 13.6 us -> 0.01 us
  starting transfers between devices: 13 us -> 0 us
  matrix products: 6.22 us -> 0 us
  local copies, waits for them, and re-layouts: 6.01 us -> 0.8 us
  other arithmetic: 4.36 us -> 0 us
    pallas_call x0 -> x1, Pallas kernels: none -> 38.9 us  [fused(): pl.pallas_call(functools.partial(kernel, rows, cols), out_shape=jax.Shape...]
    all_to_all x2 -> x0, waiting for transfers between devices: 27.3 us -> none  [the longest x1 13.7 us: body(): lax.all_to_all(product, 'row', split_axis=1, concat_axis=0, tiled=True)]
    all_to_all x1 -> x0, blocking collectives: 18.4 us -> none  [body(): lax.all_to_all(right, 'row', split_axis=0, concat_axis=1, tiled=True)]
    all_to_all x2 -> x0, starting transfers between devices: 13 us -> none  [the longest x1 7.38 us: body(): lax.all_to_all(left, 'row', split_axis=0, concat_axis=1, tiled=True)]
    dot_general x5 -> x0, matrix products: 6.22 us -> none  [the longest x2 2.69 us: branch(): jnp.einsum('kic,cd->dki', normed, weight, preferred_element_type=jnp.floa...]
    reduce_sum x4 -> x0, other arithmetic: 3.28 us -> none  [the longest x1 1.67 us: body(): variance = jnp.mean(centred * centred, axis=-1, keepdims=True)]
    all_to_all x3 -> x0, local copies, waits for them, and re-layouts: 2.91 us -> none  [the longest x2 2.88 us: body(): lax.all_to_all(left, 'row', split_axis=0, concat_axis=1, tiled=True)]
    convert_element_type x4 -> x0, local copies, waits for them, and re-layouts: 2.86 us -> none  [the longest x2 1.62 us: branch(): (jax.nn.sigmoid(projected[hidden:]) * projected[:hidden]).astype(jnp.bflo...]
  transfers between devices with their start and end apart: 3 -> 0, of which waited for: 3 -> 0; matrix products, arithmetic and copies ran while one was open for 2% -> 0% of each run, Pallas kernels for 0% -> 0%
where the time goes in v2:
time: 39.8 us; the launch traced here: 39.7 us
  Pallas kernels  38.9 us (98%)
  local copies, waits for them, and re-layouts  0.8 us (2%)
    pallas_call x1, Pallas kernels, fused(): pl.pallas_call(functools.partial(kernel, rows, cols), out_shape=jax.Shape...  38.9 us

profile of v2, /device:TPU:0, one launch (start us, length us, event | category | flops | bytes accessed | tf_op | source)
XLA Modules:
  0.0 39.7 jit_solution(4522611670442233692)
XLA Ops:
  0.0 38.9 %shard_map.91 = bf16[16,128,128]{2,1,0:T(8,128)(2,1)S(1)} custom-call(bf16[16,128,128]{2,1,0:T(8,128)(2,1)} %refs_0_.1, f32[1,128]{1,0:T(1,128)} %bitcast.4, f32[1,128]{1,0:T(1,128)} %bitcast.5, bf16[128,256]{1,0:T(8,128)(2,1)} %refs_3_.1, bf16[128,256]{1,0:T(8,128)(2,1)} %refs_4_.1, bf16[128,128]{1,0:T(8,128)(2,1)} %refs_5_.1, f32[1,128]{1,0:T(1,128)} %bitcast.6, ...), custom_call_target="tpu_custom_call" | custom-call | tf_op jit(solution)/shard_map/pallas_call | solution.py:329
  38.9 0.8 %copy.11 = bf16[16,128,128]{2,1,0:T(8,128)(2,1)} copy(bf16[16,128,128]{2,1,0:T(8,128)(2,1)S(1)} %shard_map.91) | data formatting | bytes 1048576

commit v3 on v2

--- a/solution.py
+++ b/solution.py
@@ -61,9 +61,8 @@
 
 
 MESH = pl.DeviceIdType.MESH
-CHUNKS = 4
-UNROLL = 1
-PACED = False
+CHUNKS = 8
+AHEAD = 4
 HALVES = 2
 
 
@@ -125,7 +124,7 @@
             one(half, other, lax.rem(other, half_rows), lax.div(other, half_rows))
             return carry
 
-        lax.fori_loop(1, members, step, 0, unroll=UNROLL)
+        lax.fori_loop(1, members, step, 0)
 
     def far(one):
         for away in range(1, HALVES):
@@ -140,7 +139,7 @@
                 )
                 return carry
 
-            lax.fori_loop(0, members, step, 0, unroll=UNROLL)
+            lax.fori_loop(0, members, step, 0)
 
     def everyone(one):
         far(one)
@@ -227,19 +226,17 @@
             q = m * per + t
             operands_in[q, me] = operands_out[q, me]
 
-    project(0)
-    pl.semaphore_wait(barrier, HALVES * members - 1)
-    send_operands(0)
-    if not PACED:
-        for m in range(1, CHUNKS):
-            project(m)
-            send_operands(m)
+    for m in range(AHEAD):
+        project(m)
+        if m == 0:
+            pl.semaphore_wait(barrier, HALVES * members - 1)
+        send_operands(m)
     for m in range(CHUNKS):
-        if PACED and m + 1 < CHUNKS:
-            project(m + 1)
+        if m + AHEAD < CHUNKS:
+            project(m + AHEAD)
         arrived(operands_in, m, members - 1, recv_sem)
-        if PACED and m + 1 < CHUNKS:
-            send_operands(m + 1)
+        if m + AHEAD < CHUNKS:
+            send_operands(m + AHEAD)
         for t in range(per):
             q = m * per + t
             left, right = (

time: 39.8 us -> 38.8 us (0.975)
  Pallas kernels: 38.9 us -> 37.9 us
    pallas_call x1, Pallas kernels: 38.9 us -> 37.9 us  [fused(): pl.pallas_call(functools.partial(kernel, rows, cols), out_shape=jax.Shape...]
where the time goes in v3:
time: 38.8 us; the launch traced here: 38.7 us
  Pallas kernels  37.9 us (98%)
  local copies, waits for them, and re-layouts  0.8 us (2%)
    pallas_call x1, Pallas kernels, fused(): pl.pallas_call(functools.partial(kernel, rows, cols), out_shape=jax.Shape...  37.9 us
    unnamed x1, local copies, waits for them, and re-layouts  0.8 us

profile of v3, /device:TPU:0, one launch (start us, length us, event | category | flops | bytes accessed | tf_op | source)
XLA Modules:
  0.0 38.7 jit_solution(2840408029646323448)
XLA Ops:
  0.0 37.9 %shard_map.91 = bf16[16,128,128]{2,1,0:T(8,128)(2,1)S(1)} custom-call(bf16[16,128,128]{2,1,0:T(8,128)(2,1)} %refs_0_.1, f32[1,128]{1,0:T(1,128)} %bitcast.4, f32[1,128]{1,0:T(1,128)} %bitcast.5, bf16[128,256]{1,0:T(8,128)(2,1)} %refs_3_.1, bf16[128,256]{1,0:T(8,128)(2,1)} %refs_4_.1, bf16[128,128]{1,0:T(8,128)(2,1)} %refs_5_.1, f32[1,128]{1,0:T(1,128)} %bitcast.6, ...), custom_call_target="tpu_custom_call" | custom-call | tf_op jit(solution)/shard_map/pallas_call | solution.py:326
  37.9 0.8 %copy.11 = bf16[16,128,128]{2,1,0:T(8,128)(2,1)} copy(bf16[16,128,128]{2,1,0:T(8,128)(2,1)S(1)} %shard_map.91) | data formatting | bytes 1048576
